TPU v7x, 256 devices: a whole 4x4x8 slice. The times are simulated.
256 devices in a mesh: row: 8 (over z), col: 32 (over y, x, core).
Axes of the slice: x: 4, y: 4, z: 8, core: 2. Of those that a mesh axis runs over, the one named last changes fastest.
Arguments:
- src_points: float32 [64, 32768], P(None, ('row', 'col')), may hold values from -3 to 3
- tgt_points: float32 [64, 32768], P(None, ('col', 'row')), may hold values from -0.75 to 0.75
- src_logmass: float32 [32768], P('row'), may hold values from -1 to 1
- tgt_logmass: float32 [32768], P('col'), may hold values from -1 to 1
Outputs:
- src_potential: float32 [32768], P('row')
- tgt_potential: float32 [32768], P('col')
All inputs are finite; a program needn't handle non-finite values.
Results may differ from a plain program's by a relative error of at most 0.00018.
Values sent between devices are 32-bit elements; how exact they have to be, the bound alone decides.
A program may use at most 64 MiB of HBM per device.

v0:
```python
import jax
import jax.numpy as jnp
from jax import lax
from jax.sharding import PartitionSpec as P

ITERS = 2


EPSILON = 0.05


def tile_costs(xb, xnb, yb, ynb):
    cross = lax.dot_general(
        xb,
        yb,
        (((0,), (0,)), ((), ())),
        precision=lax.Precision.HIGHEST,
        preferred_element_type=jnp.float32,
    )
    return xnb[:, None] + ynb[None, :] - 2.0 * cross


def on_device(src_points, tgt_points, src_logmass, tgt_logmass):
    source = lax.all_gather(src_points, "col", axis=1, tiled=True)
    target = lax.all_gather(tgt_points, "row", axis=1, tiled=True)
    src_norm = jnp.sum(source * source, axis=0)
    tgt_norm = jnp.sum(target * target, axis=0)
    width = source.shape[0]
    count = source.shape[1]
    tcount = target.shape[1]
    block = min(512, count)
    nblocks = count // block
    src_blocks = source.reshape(width, nblocks, block).transpose(1, 0, 2)
    src_nblocks = src_norm.reshape(nblocks, block)
    mass_blocks = src_logmass.reshape(nblocks, block)
    tgt_pot = jnp.zeros((tcount,), jnp.float32)
    src_pot = jnp.zeros((count,), jnp.float32)
    for step in range(ITERS):

        def source_rows(args):
            xb, xnb = args
            scores = (
                tgt_pot[None, :] - tile_costs(xb, xnb, target, tgt_norm)
            ) / EPSILON + tgt_logmass[None, :]
            top = jnp.max(scores, axis=1)
            return (top, jnp.sum(jnp.exp(scores - top[:, None]), axis=1))

        tops, totals = lax.map(source_rows, (src_blocks, src_nblocks))
        tops = tops.reshape(count)
        totals = totals.reshape(count)
        whole_top = lax.pmax(tops, "col")
        whole_total = lax.psum(totals * jnp.exp(tops - whole_top), "col")
        src_pot = -EPSILON * (whole_top + jnp.log(whole_total))
        pot_blocks = src_pot.reshape(nblocks, block)

        def target_step(carry, args):
            xb, xnb, fb, mb = args
            scores = (fb[:, None] - tile_costs(xb, xnb, target, tgt_norm)) / EPSILON + mb[:, None]
            run_top, run_total = carry
            new_top = jnp.maximum(run_top, jnp.max(scores, axis=0))
            new_total = run_total * jnp.exp(run_top - new_top) + jnp.sum(
                jnp.exp(scores - new_top[None, :]), axis=0
            )
            return ((new_top, new_total), None)

        start = (jnp.full((tcount,), -jnp.inf, jnp.float32), jnp.zeros((tcount,), jnp.float32))
        (col_top, col_total), unused = lax.scan(
            target_step, start, (src_blocks, src_nblocks, pot_blocks, mass_blocks)
        )
        all_top = lax.pmax(col_top, "row")
        all_total = lax.psum(col_total * jnp.exp(col_top - all_top), "row")
        tgt_pot = -EPSILON * (all_top + jnp.log(all_total))
    return (src_pot, tgt_pot)


def solution(mesh):
    return jax.shard_map(
        on_device,
        mesh=mesh,
        in_specs=(P(None, ("row", "col")), P(None, ("col", "row")), P("row"), P("col")),
        out_specs=(P("row"), P("col")),
        check_vma=False,
    )
```

profile of v0, /device:TPU:1, one launch (start us, length us, event | category | flops | bytes accessed | tf_op | source)
XLA Modules:
  0.0 714.2 jit_solution(10854024081702996067)
XLA Ops:
  8.7 23.5 %all_gather.7 = f32[64,1024]{1,0:T(8,128)S(1)} all-gather(f32[64,128]{1,0:T(8,128)} %param.13), channel_id=1, replica_groups=mesh['row'=8,'col'=32] {'row'}, dimensions={1}, use_global_device_ids=true | all-gather | bytes 294912 | tf_op jit(solution)/shard_map/all_gather | solution.py:25
  32.2 30.5 %all-gather.2.cloned.1.call-done = f32[64,4096]{1,0:T(8,128)} async-done(((f32[64,128]{1,0:T(8,128)}), f32[64,4096]{1,0:T(8,128)}) %all-gather.2.cloned.1.call-update) | async-done | bytes 1048592 | tf_op jit(solution)/shard_map/all_gather | solution.py:24
  65.4 24.5 %while.50 = (s32[]{:T(128)}, f32[8,512]{1,0:T(8,128)S(1)}, f32[8,512]{1,0:T(8,128)S(1)}, f32[8,512]{1,0:T(8,128)S(1)}, f32[1024]{0:T(1024)S(1)}, /*index=5*/f32[...) while((s32[]{:T(128)}, f32[8,512]{1,0:T(8,128)S(1)}, ...), condition=%wide.region_5.6_spmd, body=%wide.region_2.5_spmd.sunk | while | flops 407370752 | bytes 4616309 | solution.py:48
  65.5 2.4 fusion.33
  68.5 2.4 fusion.33
  71.6 2.4 fusion.33
  74.6 2.4 fusion.33
  77.7 2.4 fusion.33
  80.8 2.4 fusion.33
  83.8 2.4 fusion.33
  86.9 2.4 fusion.33
  90.0 120.9 %pmax.28 = f32[4096]{0:T(1024)S(1)} all-reduce(f32[4096]{0:T(1024)S(1)} %bitcast.94), channel_id=1, replica_groups=mesh['row'=8,'col'=32] {'col'}, use_global_device_ids=true, to_apply=%region_6.7 | all-reduce | flops 4096 | bytes 32768 | tf_op jit(solution)/shard_map/pmax | solution.py:51
  210.9 123.8 %psum.28 = f32[4096]{0:T(1024)S(1)} all-reduce(f32[4096]{0:T(1024)S(1)} %exponential_multiply_fusion.1), channel_id=1, replica_groups=mesh['row'=8,'col'=32] {'col'}, use_global_device_ids=true, to_apply=%region_7.8 | all-reduce | flops 4096 | bytes 32768 | tf_op jit(solution)/shard_map/psum | solution.py:52
  334.7 21.7 %while.52 = (s32[]{:T(128)}, f32[1024]{0:T(1024)S(1)}, f32[1024]{0:T(1024)S(1)}, f32[8,512]{1,0:T(8,128)S(1)}, f32[8,512]{1,0:T(8,128)S(1)}, /*index=5*/f32[1024...) while((s32[]{:T(128)}, f32[1024]{0:T(1024)S(1)}, ...), condition=%wide.region_11.12_spmd.clone, body=%wide.region_8.11_spmd.clone.sunk | while | flops 407376896 | bytes 4663428 | solution.py:67
  337.4 2.3 fusion.37
  356.4 13.7 %pmax.29 = f32[1024]{0:T(1024)S(1)} all-reduce(f32[1024]{0:T(1024)S(1)} %get-tuple-element.191), channel_id=1, replica_groups=mesh['row'=8,'col'=32] {'row'}, use_global_device_ids=true, to_apply=%region_12.13 | all-reduce | flops 1024 | bytes 8192 | tf_op jit(solution)/shard_map/pmax | solution.py:70
  370.1 11.6 %psum.29 = f32[1024]{0:T(1024)S(1)} all-reduce(f32[1024]{0:T(1024)S(1)} %exponential_multiply_fusion.3), channel_id=1, replica_groups=mesh['row'=8,'col'=32] {'row'}, use_global_device_ids=true, to_apply=%region_13.14 | all-reduce | flops 1024 | bytes 8192 | tf_op jit(solution)/shard_map/psum | solution.py:71
  381.7 24.6 %while.51 = (s32[]{:T(128)}, f32[8,512]{1,0:T(8,128)S(1)}, f32[8,512]{1,0:T(8,128)S(1)}, f32[1024]{0:T(1024)S(1)}, f32[8,512]{1,0:T(8,128)S(1)}, /*index=5*/f32[...) while((s32[]{:T(128)}, f32[8,512]{1,0:T(8,128)S(1)}, ...), condition=%wide.region_17.18_spmd, body=%wide.region_14.17_spmd.sunk | while | flops 407370752 | bytes 4620413 | solution.py:48
  381.7 2.4 fusion.35
  384.8 2.4 fusion.35
  387.9 2.4 fusion.35
  391.0 2.4 fusion.35
  394.0 2.4 fusion.35
  397.1 2.4 fusion.35
  400.2 2.4 fusion.35
  403.2 2.4 fusion.35
  406.3 131.0 %pmax.30 = f32[4096]{0:T(1024)S(1)} all-reduce(f32[4096]{0:T(1024)S(1)} %bitcast.96), channel_id=1, replica_groups=mesh['row'=8,'col'=32] {'col'}, use_global_device_ids=true, to_apply=%region_18.19 | all-reduce | flops 4096 | bytes 32768 | tf_op jit(solution)/shard_map/pmax | solution.py:51
  537.3 124.0 %psum.30 = f32[4096]{0:T(1024)S(1)} all-reduce(f32[4096]{0:T(1024)S(1)} %exponential_multiply_fusion), channel_id=1, replica_groups=mesh['row'=8,'col'=32] {'col'}, use_global_device_ids=true, to_apply=%region_19.20 | all-reduce | flops 4096 | bytes 32768 | tf_op jit(solution)/shard_map/psum | solution.py:52
  661.9 21.7 %while.53 = (s32[]{:T(128)}, f32[1024]{0:T(1024)S(1)}, f32[1024]{0:T(1024)S(1)}, f32[8,512]{1,0:T(8,128)S(1)}, f32[8,512]{1,0:T(8,128)S(1)}, /*index=5*/f32[1024...) while((s32[]{:T(128)}, f32[1024]{0:T(1024)S(1)}, ...), condition=%wide.region_23.24_spmd.clone, body=%wide.region_20.23_spmd.clone.sunk | while | flops 407376896 | bytes 4663428 | solution.py:67
  678.2 2.3 fusion.40
  683.6 11.6 %pmax.31 = f32[1024]{0:T(1024)S(1)} all-reduce(f32[1024]{0:T(1024)S(1)} %get-tuple-element.195), channel_id=1, replica_groups=mesh['row'=8,'col'=32] {'row'}, use_global_device_ids=true, to_apply=%region_24.25 | all-reduce | flops 1024 | bytes 8192 | tf_op jit(solution)/shard_map/pmax | solution.py:70
  695.2 11.6 %psum.31 = f32[1024]{0:T(1024)S(1)} all-reduce(f32[1024]{0:T(1024)S(1)} %exponential_multiply_fusion.2), channel_id=1, replica_groups=mesh['row'=8,'col'=32] {'row'}, use_global_device_ids=true, to_apply=%region_25.26 | all-reduce | flops 1024 | bytes 8192 | tf_op jit(solution)/shard_map/psum | solution.py:71
  (210 shorter events, 53.6 us)
Async XLA Ops:
  7.2 55.5 %all-gather.2.cloned.1.call-start = ((), (), s32[]{:S(2)}) async-start(), calls=%async_computation | async-start | bytes 1081344 | tf_op jit(solution)/shard_map/all_gather | solution.py:24
  62.7 2.6 copy-start
  64.6 0.8 copy-start.2
  661.3 0.6 copy-start.1
Sparse Core Ops, SparseCore 0:
  10.5 52.1 all-gather.1
where the time goes:
time: 725 us; the launch traced here: 714 us
  blocking collectives  571 us (79%)
  matrix products  74.9 us (10%)
  waiting for transfers between devices  31.2 us (4%)
  other arithmetic  14.6 us (2%)
  between operations  14.2 us (2%)
    pmax x2, blocking collectives, on_device(): whole_top = lax.pmax(tops, 'col')  252 us
    psum x2, blocking collectives, on_device(): whole_total = lax.psum(totals * jnp.exp(tops - whole_top), 'col')  248 us
    dot_general x32, matrix products, tile_costs(): lax.dot_general(xb, yb, (((0,), (0,)), ((), ())), precision=lax.Precision...  74.9 us
    all_gather x1, waiting for transfers between devices, on_device(): source = lax.all_gather(src_points, 'col', axis=1, tiled=True)  30.5 us
    pmax x2, blocking collectives, on_device(): all_top = lax.pmax(col_top, 'row')  25.3 us
    all_gather x1, blocking collectives, on_device(): target = lax.all_gather(tgt_points, 'row', axis=1, tiled=True)  23.5 us
    psum x2, blocking collectives, on_device(): all_total = lax.psum(col_total * jnp.exp(col_top - all_top), 'row')  23.2 us
  transfers between devices with their start and end apart: 1, of which 1 were waited for; matrix products, arithmetic and copies ran while one was open for 0% of the time, Pallas kernels for 0%

commit v1 on v0

v1 whole, which is shorter than its diff:
```python
import functools
import math

import jax
import jax.numpy as jnp
from jax import lax
from jax.experimental import pallas as pl
from jax.experimental.pallas import tpu as pltpu
from jax.sharding import PartitionSpec as P

MESH = pl.DeviceIdType.MESH
EPSILON = 0.05
LOG2E = math.log2(math.e)
SCORE = LOG2E / EPSILON
UNIT = EPSILON / LOG2E
D = 64
B = 128
NB = 16
N = NB * B
F32 = jnp.float32
BF16 = jnp.bfloat16

PLANE = sorted(
    [(dy, dx) for dy in range(4) for dx in range(4) if (dy, dx) != (0, 0)],
    key=lambda o: min(o[0], 4 - o[0]) + min(o[1], 4 - o[1]),
)
RING = sorted(range(1, 8), key=lambda d: min(d, 8 - d))
COLUMN = sorted(
    [(dz, dc) for dz in range(8) for dc in range(2) if (dz, dc) != (0, 0)],
    key=lambda o: min(o[0], 8 - o[0]),
)


def lse_rows(values):
    top = jnp.max(values, axis=0)
    return top + jnp.log(jnp.sum(jnp.exp2(values - top[None]), axis=0)) * LOG2E


def kernel(
    x_ref, y_ref, a_ref, b_ref, f_ref, g_ref,
    xs, ys, bfull, X, Y, T, xn, yn, gb, fa, fb8, mbuf, sbuf, R8, v8,
    ex1, ex2, ex3, ex4, fsib,
    x_send, x_recv, y_send, y_recv, p_send, p_recv, b_sem, e_send, e_recv, f_sem,
):
    z = lax.axis_index("row")
    c = lax.axis_index("col")
    core = lax.rem(c, 2)
    chip = lax.div(c, 2)
    xi = lax.rem(chip, 4)
    yi = lax.div(chip, 4)
    here = core * 8 + z

    def plane(o):
        dy, dx = o
        return (z, (lax.rem(yi + dy, 4) * 4 + lax.rem(xi + dx, 4)) * 2 + core)

    def column(o):
        dz, dc = o
        return (lax.rem(z + dz, 8), chip * 2 + lax.rem(core + dc, 2))

    sibling = column((0, 1))

    def send(src, dst, ssem, rsem, dev):
        copy = pltpu.make_async_remote_copy(
            src_ref=src, dst_ref=dst, send_sem=ssem, recv_sem=rsem, device_id=dev, device_id_type=MESH
        )
        copy.start()

    def wait(ref, sem):
        pltpu.make_async_copy(ref, ref, sem).wait()

    barrier = pltpu.get_barrier_semaphore()
    for o in PLANE:
        pl.semaphore_signal(barrier, inc=1, device_id=plane(o), device_id_type=MESH)
    for o in COLUMN:
        pl.semaphore_signal(barrier, inc=1, device_id=column(o), device_id_type=MESH)
    xs[chip] = x_ref[...]
    ys[here] = y_ref[...]
    mine8 = pl.ds(pl.multiple_of(core * 8, 8), 8)
    bfull[mine8, :] = b_ref[...]
    pl.semaphore_wait(barrier, len(PLANE) + len(COLUMN))

    for k, dz in enumerate(RING):
        send(ys.at[here], ys.at[here], y_send, y_recv.at[k], column((dz, 0)))
    send(ys.at[here], ys.at[here], p_send, p_recv.at[7], sibling)
    send(bfull.at[mine8], bfull.at[mine8], b_sem.at[0], b_sem.at[1], sibling)
    for k, o in enumerate(PLANE):
        send(xs.at[chip], xs.at[chip], x_send, x_recv.at[k], plane(o))
    for k, dz in enumerate(RING):
        slot = core * 8 + lax.rem(z + 8 - dz, 8)
        wait(ys.at[slot], y_recv.at[k])
        send(ys.at[slot], ys.at[slot], p_send, p_recv.at[k], sibling)
    for k, o in enumerate(PLANE):
        wait(xs.at[0], x_recv.at[k])

    ones = (lax.broadcasted_iota(jnp.int32, (D, B), 0) < 3).astype(BF16)

    def build_source(m, _):
        x = xs[m]
        xn[pl.ds(m, 1), :] = jnp.sum(x * x, axis=0, keepdims=True)
        scaled = x * (2.0 * SCORE)
        hi = scaled.astype(BF16)
        lo = (scaled - hi.astype(F32)).astype(BF16)
        at = pl.ds(pl.multiple_of(m * B, B), B)
        X[0:64, at] = hi
        X[64:128, at] = ones
        X[128:192, at] = hi
        X[192:256, at] = lo
        return 0

    lax.fori_loop(0, NB, build_source, 0)

    for k in range(8):
        wait(ys.at[0], p_recv.at[k])
    wait(bfull.at[mine8], b_sem.at[1])

    left = lax.broadcasted_iota(jnp.int32, (B, B), 1) < D

    def build_target(t, _):
        y = ys[t]
        norm = jnp.sum(y * y, axis=0, keepdims=True)
        yn[pl.ds(t, 1), :] = norm
        bias = bfull[pl.ds(t, 1), :] * LOG2E - norm * SCORE
        gb[pl.ds(t, 1), :] = bias
        hi = bias.astype(BF16).astype(F32)
        mid = (bias - hi).astype(BF16).astype(F32)
        lo = bias - hi - mid
        row = lax.broadcasted_iota(jnp.int32, (D, B), 0)
        tail = jnp.where(row == 0, hi, jnp.where(row == 1, mid, jnp.where(row == 2, lo, 0.0)))
        both = jnp.concatenate([y, tail], axis=0).T
        top = both.astype(BF16).astype(F32)
        rest = jnp.where(left, both - top, pltpu.roll(top, D, 1))
        at = pl.ds(pl.multiple_of(t * B, B), B)
        Y[at, 0:128] = top.astype(BF16)
        Y[at, 128:256] = rest.astype(BF16)
        return 0

    lax.fori_loop(0, NB, build_target, 0)

    def half1(n, _):
        at = pl.ds(pl.multiple_of(n * 256, 256), 256)
        T[:, at] = jnp.dot(Y[...], X[:, at], preferred_element_type=F32)
        for u in range(2):
            lane = pl.ds(pl.multiple_of(n * 256 + u * B, B), B)

            def strip(q, carry):
                m, s = carry
                rows = T[pl.ds(pl.multiple_of(q * 128, 128), 128), lane].reshape(16, 8, B)
                new = jnp.maximum(m, jnp.max(rows, axis=0))
                s = s * jnp.exp2(m - new) + jnp.sum(jnp.exp2(rows - new[None]), axis=0)
                return new, s

            m, s = lax.fori_loop(
                0, NB, strip, (jnp.full((8, B), -1e30, F32), jnp.zeros((8, B), F32))
            )
            top = jnp.max(m, axis=0, keepdims=True)
            total = jnp.sum(s * jnp.exp2(m - top), axis=0, keepdims=True)
            ex1[chip, pl.ds(n * 2 + u, 1), :] = top + jnp.log(total) * LOG2E
        return 0

    lax.fori_loop(0, 8, half1, 0)

    def exchange(ex, mine, targets, e):
        for o in reversed(targets):
            send(ex.at[mine], ex.at[mine], e_send.at[e], e_recv.at[e], o)
        wait(ex.at[pl.ds(0, 15)], e_recv.at[e])

    planes = [plane(o) for o in PLANE]
    columns = [column(o) for o in COLUMN]

    exchange(ex1, chip, planes, 0)
    a2 = a_ref[pl.ds(core, NB, stride=2), :] * LOG2E
    first = a2 - lse_rows(ex1[...])
    fa[...] = first
    for n in range(NB):
        fb8[:, n * B : (n + 1) * B] = jnp.broadcast_to(fa[n : n + 1, :], (8, B))

    def half2(t, _):
        def strip(q, _):
            at = pl.ds(pl.multiple_of(t * B + q * 8, 8), 8)
            parts = []
            for n in range(NB):
                lane = slice(n * B, (n + 1) * B)
                value = T[at, lane] + fb8[:, lane]
                T[at, lane] = value
                parts.append(value)
            tops = parts
            while len(tops) > 1:
                tops = [jnp.maximum(p, q) for p, q in zip(tops[::2], tops[1::2])]
            sums = [jnp.exp2(p - tops[0]) for p in parts]
            while len(sums) > 1:
                sums = [p + q for p, q in zip(sums[::2], sums[1::2])]
            at = pl.ds(pl.multiple_of(q * 8, 8), 8)
            mbuf[at, :] = tops[0]
            sbuf[at, :] = sums[0]
            return 0

        lax.fori_loop(0, NB, strip, 0)
        m = mbuf[...].T
        s = sbuf[...].T
        top = jnp.max(m, axis=0, keepdims=True)
        total = jnp.sum(s * jnp.exp2(m - top), axis=0, keepdims=True)
        ex2[here, pl.ds(t, 1), :] = top + jnp.log(total) * LOG2E
        return 0

    lax.fori_loop(0, NB, half2, 0)
    exchange(ex2, here, columns, 1)
    b2 = bfull[...] * LOG2E
    total2 = lse_rows(ex2[...])
    gb[...] = gb[...] - total2 + b2
    fa[...] = b2 - total2

    R8[...] = jnp.zeros((8, N), F32)

    def half3(t, _):
        mbuf[...] = jnp.broadcast_to(fa[pl.ds(t, 1), :], (B, B)).T

        def strip(q, _):
            at = pl.ds(pl.multiple_of(t * B + q * 8, 8), 8)
            shift = mbuf[pl.ds(pl.multiple_of(q * 8, 8), 8), :]
            for n in range(NB):
                lane = slice(n * B, (n + 1) * B)
                value = jnp.exp2(T[at, lane] + shift)
                T[at, lane] = value
                R8[:, lane] = R8[:, lane] + value
            return 0

        lax.fori_loop(0, NB, strip, 0)
        return 0

    lax.fori_loop(0, NB, half3, 0)
    for n in range(NB):
        ex3[chip, n : n + 1, :] = jnp.sum(R8[:, n * B : (n + 1) * B], axis=0, keepdims=True)
    exchange(ex3, chip, planes, 2)
    total3 = jnp.sum(ex3[...], axis=0)
    second = first - jnp.log(total3) * LOG2E
    fsib[0] = xn[...] + second * UNIT
    send(fsib.at[0], fsib.at[1], f_sem.at[0], f_sem.at[1], sibling)
    fa[...] = jnp.exp2(a2) / total3
    for n in range(NB):
        v8[:, n * B : (n + 1) * B] = jnp.broadcast_to(fa[n : n + 1, :], (8, B))

    def half4(t, _):
        def strip(q, _):
            at = pl.ds(pl.multiple_of(t * B + q * 8, 8), 8)
            sums = []
            for n in range(NB):
                lane = slice(n * B, (n + 1) * B)
                sums.append(T[at, lane] * v8[:, lane])
            while len(sums) > 1:
                sums = [p + q for p, q in zip(sums[::2], sums[1::2])]
            sbuf[pl.ds(pl.multiple_of(q * 8, 8), 8), :] = sums[0]
            return 0

        lax.fori_loop(0, NB, strip, 0)
        ex4[here, pl.ds(t, 1), :] = jnp.sum(sbuf[...].T, axis=0, keepdims=True)
        return 0

    lax.fori_loop(0, NB, half4, 0)
    exchange(ex4, here, columns, 3)
    total4 = jnp.sum(ex4[...], axis=0)
    fa[...] = yn[...] + (gb[...] - jnp.log(total4) * LOG2E) * UNIT
    g_ref[...] = fa[mine8, :]
    wait(fsib.at[1], f_sem.at[1])
    f_ref[pl.ds(core, NB, stride=2), :] = fsib[0]
    f_ref[pl.ds(1 - core, NB, stride=2), :] = fsib[1]

    wait(xs.at[pl.ds(0, 15)], x_send)
    wait(ys.at[pl.ds(0, 7)], y_send)
    wait(ys.at[pl.ds(0, 8)], p_send)
    wait(bfull.at[mine8], b_sem.at[0])
    wait(fsib.at[0], f_sem.at[0])
    for e, ex in enumerate((ex1, ex2, ex3, ex4)):
        wait(ex.at[pl.ds(0, 15)], e_send.at[e])


def on_device(src_points, tgt_points, src_logmass, tgt_logmass):
    vmem = pl.BlockSpec(memory_space=pltpu.VMEM)
    dma = pltpu.SemaphoreType.DMA
    exchange = pltpu.VMEM((NB, NB, B), F32)
    f, g = pl.pallas_call(
        kernel,
        out_shape=(jax.ShapeDtypeStruct((32, B), F32), jax.ShapeDtypeStruct((8, B), F32)),
        in_specs=[vmem] * 4,
        out_specs=(vmem, vmem),
        scratch_shapes=[
            pltpu.VMEM((NB, D, B), F32),
            pltpu.VMEM((NB, D, B), F32),
            pltpu.VMEM((NB, B), F32),
            pltpu.VMEM((256, N), BF16),
            pltpu.VMEM((N, 256), BF16),
            pltpu.VMEM((N, N), F32),
            pltpu.VMEM((NB, B), F32),
            pltpu.VMEM((NB, B), F32),
            pltpu.VMEM((NB, B), F32),
            pltpu.VMEM((NB, B), F32),
            pltpu.VMEM((8, N), F32),
            pltpu.VMEM((B, B), F32),
            pltpu.VMEM((B, B), F32),
            pltpu.VMEM((8, N), F32),
            pltpu.VMEM((8, N), F32),
            exchange, exchange, exchange, exchange,
            pltpu.VMEM((2, NB, B), F32),
            dma, dma((15,)), dma, dma((7,)), dma, dma((8,)), dma((2,)), dma((4,)), dma((4,)), dma((2,)),
        ],
        compiler_params=pltpu.CompilerParams(
            collective_id=0, has_side_effects=True, vmem_limit_bytes=56 << 20
        ),
    )(src_points, tgt_points, src_logmass.reshape(32, B), tgt_logmass.reshape(8, B))
    return f.reshape(-1), g.reshape(-1)


def solution(mesh):
    return jax.shard_map(
        on_device,
        mesh=mesh,
        in_specs=(P(None, ("row", "col")), P(None, ("col", "row")), P("row"), P("col")),
        out_specs=(P("row"), P("col")),
        check_vma=False,
    )
```

time: 725 us -> 83.2 us (0.11); the launches traced: 714 us -> 83 us
  blocking collectives: 571 us -> 0 us
  Pallas kernels: 0 us -> 80.5 us
  matrix products: 74.9 us -> 0 us
  waiting for transfers between devices: 31.2 us -> 0 us
  other arithmetic: 14.6 us -> 0 us
  between operations: 14.2 us -> 0.65 us
    pmax x4 -> x0, blocking collectives: 277 us -> none  [the longest x2 252 us: on_device(): whole_top = lax.pmax(tops, 'col')]
    psum x4 -> x0, blocking collectives: 271 us -> none  [the longest x2 248 us: on_device(): whole_total = lax.psum(totals * jnp.exp(tops - whole_top), 'col')]
    pallas_call x0 -> x1, Pallas kernels: none -> 80.5 us  [on_device(): pl.pallas_call(kernel, out_shape=(jax.ShapeDtypeStruct((32, B), F32), jax...]
    dot_general x32 -> x0, matrix products: 74.9 us -> none  [tile_costs(): lax.dot_general(xb, yb, (((0,), (0,)), ((), ())), precision=lax.Precision...]
    all_gather x1 -> x0, waiting for transfers between devices: 30.5 us -> none  [on_device(): source = lax.all_gather(src_points, 'col', axis=1, tiled=True)]
    all_gather x1 -> x0, blocking collectives: 23.5 us -> none  [on_device(): target = lax.all_gather(tgt_points, 'row', axis=1, tiled=True)]
    reduce_sum x34 -> x0, other arithmetic: 13.6 us -> none  [the longest x16 8.25 us: source_rows(): return (top, jnp.sum(jnp.exp(scores - top[:, None]), axis=1))]
  transfers between devices with their start and end apart: 1 -> 0, of which waited for: 1 -> 0; matrix products, arithmetic and copies ran while one was open for 0% -> 0% of each run, Pallas kernels for 0% -> 0%
where the time goes in v1:
time: 83.2 us; the launch traced here: 83 us
  Pallas kernels  80.5 us (97%)
  local copies, waits for them, and re-layouts  1.92 us (2%)
    pallas_call x1, Pallas kernels, on_device(): pl.pallas_call(kernel, out_shape=(jax.ShapeDtypeStruct((32, B), F32), jax...  80.5 us
    unnamed x4, local copies, waits for them, and re-layouts  1.92 us

profile of v1, /device:TPU:1, one launch (start us, length us, event | category | flops | bytes accessed | tf_op | source)
XLA Modules:
  0.0 83.0 jit_solution(15193293480480405738)
XLA Ops:
  0.6 80.5 %shard_map.59 = (f32[32,128]{1,0:T(8,128)}, f32[8,128]{1,0:T(8,128)}) custom-call(f32[64,128]{1,0:T(8,128)} %x_ref.1, f32[64,128]{1,0:T(8,128)} %y_ref.1, f32[32,128]{1,0:T(8,128)} %bitcast.5, f32[8,128]{1,0:T(8,128)} %bitcast.7), custom_call_target="tpu_custom_call" | custom-call | tf_op jit(solution)/shard_map/pallas_call | solution.py:281
  81.1 0.0 copy-start
  81.1 1.3 %copy.8 = f32[4096]{0:T(1024)} copy(f32[4096]{0:T(1024)} %bitcast.4) | data formatting | bytes 32768
  82.4 0.0 copy-done
  82.4 0.6 copy.9
Async XLA Ops:
  81.1 1.3 %copy-start = (f32[8,128]{1,0:T(8,128)S(1)}, f32[8,128]{1,0:T(8,128)}, u32[]{:S(2)}) copy-start(f32[8,128]{1,0:T(8,128)} %get-tuple-element.5) | copy-start | bytes 12292

commit v2 on v1

--- a/solution.py
+++ b/solution.py
@@ -34,6 +34,12 @@
 def lse_rows(values):
     top = jnp.max(values, axis=0)
     return top + jnp.log(jnp.sum(jnp.exp2(values - top[None]), axis=0)) * LOG2E
+
+
+def tree(op, parts):
+    while len(parts) > 1:
+        parts = [op(p, q) for p, q in zip(parts[::2], parts[1::2])]
+    return parts[0]
 
 
 def kernel(
@@ -117,6 +123,11 @@
     left = lax.broadcasted_iota(jnp.int32, (B, B), 1) < D
 
     def build_target(t, _):
+        for q in range(4):
+            build_one(t * 4 + q)
+        return 0
+
+    def build_one(t):
         y = ys[t]
         norm = jnp.sum(y * y, axis=0, keepdims=True)
         yn[pl.ds(t, 1), :] = norm
@@ -133,26 +144,23 @@
         at = pl.ds(pl.multiple_of(t * B, B), B)
         Y[at, 0:128] = top.astype(BF16)
         Y[at, 128:256] = rest.astype(BF16)
-        return 0
-
-    lax.fori_loop(0, NB, build_target, 0)
+
+    lax.fori_loop(0, 4, build_target, 0)
 
     def half1(n, _):
         at = pl.ds(pl.multiple_of(n * 256, 256), 256)
         T[:, at] = jnp.dot(Y[...], X[:, at], preferred_element_type=F32)
         for u in range(2):
             lane = pl.ds(pl.multiple_of(n * 256 + u * B, B), B)
-
-            def strip(q, carry):
-                m, s = carry
-                rows = T[pl.ds(pl.multiple_of(q * 128, 128), 128), lane].reshape(16, 8, B)
-                new = jnp.maximum(m, jnp.max(rows, axis=0))
-                s = s * jnp.exp2(m - new) + jnp.sum(jnp.exp2(rows - new[None]), axis=0)
-                return new, s
-
-            m, s = lax.fori_loop(
-                0, NB, strip, (jnp.full((8, B), -1e30, F32), jnp.zeros((8, B), F32))
-            )
+            m = s = None
+            for q in range(NB):
+                rows = [T[q * B + r * 8 : q * B + r * 8 + 8, lane] for r in range(16)]
+                new = tree(jnp.maximum, rows)
+                if q:
+                    new = jnp.maximum(m, new)
+                total = tree(jnp.add, [jnp.exp2(r - new) for r in rows])
+                s = total + s * jnp.exp2(m - new) if q else total
+                m = new
             top = jnp.max(m, axis=0, keepdims=True)
             total = jnp.sum(s * jnp.exp2(m - top), axis=0, keepdims=True)
             ex1[chip, pl.ds(n * 2 + u, 1), :] = top + jnp.log(total) * LOG2E
@@ -176,34 +184,34 @@
         fb8[:, n * B : (n + 1) * B] = jnp.broadcast_to(fa[n : n + 1, :], (8, B))
 
     def half2(t, _):
-        def strip(q, _):
-            at = pl.ds(pl.multiple_of(t * B + q * 8, 8), 8)
+        block = pl.ds(pl.multiple_of(t * B, B), B)
+        Tb, mb, sb = T.at[block], mbuf.at[block], sbuf.at[block]
+        for q in range(NB):
+            at = slice(q * 8, q * 8 + 8)
             parts = []
             for n in range(NB):
                 lane = slice(n * B, (n + 1) * B)
-                value = T[at, lane] + fb8[:, lane]
-                T[at, lane] = value
+                value = Tb[at, lane] + fb8[:, lane]
+                Tb[at, lane] = value
                 parts.append(value)
-            tops = parts
-            while len(tops) > 1:
-                tops = [jnp.maximum(p, q) for p, q in zip(tops[::2], tops[1::2])]
-            sums = [jnp.exp2(p - tops[0]) for p in parts]
-            while len(sums) > 1:
-                sums = [p + q for p, q in zip(sums[::2], sums[1::2])]
-            at = pl.ds(pl.multiple_of(q * 8, 8), 8)
-            mbuf[at, :] = tops[0]
-            sbuf[at, :] = sums[0]
-            return 0
-
-        lax.fori_loop(0, NB, strip, 0)
-        m = mbuf[...].T
-        s = sbuf[...].T
-        top = jnp.max(m, axis=0, keepdims=True)
-        total = jnp.sum(s * jnp.exp2(m - top), axis=0, keepdims=True)
-        ex2[here, pl.ds(t, 1), :] = top + jnp.log(total) * LOG2E
+            top = tree(jnp.maximum, parts)
+            mb[at, :] = top
+            sb[at, :] = tree(jnp.add, [jnp.exp2(p - top) for p in parts])
         return 0
 
     lax.fori_loop(0, NB, half2, 0)
+
+    def join2(t, _):
+        for q in range(4):
+            at = pl.ds(pl.multiple_of(t * 4 * B, B) + q * B, B)
+            m = mbuf[at, :].T
+            s = sbuf[at, :].T
+            top = jnp.max(m, axis=0, keepdims=True)
+            total = jnp.sum(s * jnp.exp2(m - top), axis=0, keepdims=True)
+            ex2[here, pl.ds(t * 4 + q, 1), :] = top + jnp.log(total) * LOG2E
+        return 0
+
+    lax.fori_loop(0, 4, join2, 0)
     exchange(ex2, here, columns, 1)
     b2 = bfull[...] * LOG2E
     total2 = lse_rows(ex2[...])
@@ -212,20 +220,28 @@
 
     R8[...] = jnp.zeros((8, N), F32)
 
+    def spread(t, _):
+        for q in range(4):
+            at = pl.ds(pl.multiple_of(t * 4 * B, B) + q * B, B)
+            mbuf[at, :] = jnp.broadcast_to(fa[pl.ds(t * 4 + q, 1), :], (B, B)).T
+        return 0
+
+    lax.fori_loop(0, 4, spread, 0)
+
     def half3(t, _):
-        mbuf[...] = jnp.broadcast_to(fa[pl.ds(t, 1), :], (B, B)).T
-
-        def strip(q, _):
-            at = pl.ds(pl.multiple_of(t * B + q * 8, 8), 8)
-            shift = mbuf[pl.ds(pl.multiple_of(q * 8, 8), 8), :]
+        block = pl.ds(pl.multiple_of(t * B, B), B)
+        Tb, mb = T.at[block], mbuf.at[block]
+        for h in range(2):
+            ats = [slice((h * 8 + q) * 8, (h * 8 + q) * 8 + 8) for q in range(8)]
+            shifts = [mb[at, :] for at in ats]
             for n in range(NB):
                 lane = slice(n * B, (n + 1) * B)
-                value = jnp.exp2(T[at, lane] + shift)
-                T[at, lane] = value
-                R8[:, lane] = R8[:, lane] + value
-            return 0
-
-        lax.fori_loop(0, NB, strip, 0)
+                values = []
+                for at, shift in zip(ats, shifts):
+                    value = jnp.exp2(Tb[at, lane] + shift)
+                    Tb[at, lane] = value
+                    values.append(value)
+                R8[:, lane] = R8[:, lane] + tree(jnp.add, values)
         return 0
 
     lax.fori_loop(0, NB, half3, 0)
@@ -241,22 +257,30 @@
         v8[:, n * B : (n + 1) * B] = jnp.broadcast_to(fa[n : n + 1, :], (8, B))
 
     def half4(t, _):
-        def strip(q, _):
-            at = pl.ds(pl.multiple_of(t * B + q * 8, 8), 8)
-            sums = []
+        block = pl.ds(pl.multiple_of(t * B, B), B)
+        Tb, sb = T.at[block], sbuf.at[block]
+        for h in range(2):
+            ats = [slice((h * 8 + q) * 8, (h * 8 + q) * 8 + 8) for q in range(8)]
+            sums = [None] * 8
             for n in range(NB):
                 lane = slice(n * B, (n + 1) * B)
-                sums.append(T[at, lane] * v8[:, lane])
-            while len(sums) > 1:
-                sums = [p + q for p, q in zip(sums[::2], sums[1::2])]
-            sbuf[pl.ds(pl.multiple_of(q * 8, 8), 8), :] = sums[0]
-            return 0
-
-        lax.fori_loop(0, NB, strip, 0)
-        ex4[here, pl.ds(t, 1), :] = jnp.sum(sbuf[...].T, axis=0, keepdims=True)
+                weight = v8[:, lane]
+                for q, at in enumerate(ats):
+                    value = Tb[at, lane] * weight
+                    sums[q] = value if n == 0 else sums[q] + value
+            for q, at in enumerate(ats):
+                sb[at, :] = sums[q]
         return 0
 
     lax.fori_loop(0, NB, half4, 0)
+
+    def join4(t, _):
+        for q in range(4):
+            at = pl.ds(pl.multiple_of(t * 4 * B, B) + q * B, B)
+            ex4[here, pl.ds(t * 4 + q, 1), :] = jnp.sum(sbuf[at, :].T, axis=0, keepdims=True)
+        return 0
+
+    lax.fori_loop(0, 4, join4, 0)
     exchange(ex4, here, columns, 3)
     total4 = jnp.sum(ex4[...], axis=0)
     fa[...] = yn[...] + (gb[...] - jnp.log(total4) * LOG2E) * UNIT
@@ -295,8 +319,8 @@
             pltpu.VMEM((NB, B), F32),
             pltpu.VMEM((NB, B), F32),
             pltpu.VMEM((8, N), F32),
-            pltpu.VMEM((B, B), F32),
-            pltpu.VMEM((B, B), F32),
+            pltpu.VMEM((N, B), F32),
+            pltpu.VMEM((N, B), F32),
             pltpu.VMEM((8, N), F32),
             pltpu.VMEM((8, N), F32),
             exchange, exchange, exchange, exchange,

time: 83.2 us -> 61.3 us (0.74)
  Pallas kernels: 80.5 us -> 58.6 us
    pallas_call x1, Pallas kernels: 80.5 us -> 58.6 us  [on_device(): pl.pallas_call(kernel, out_shape=(jax.ShapeDtypeStruct((32, B), F32), jax...]
where the time goes in v2:
time: 61.3 us; the launch traced here: 61.1 us
  Pallas kernels  58.6 us (96%)
  local copies, waits for them, and re-layouts  1.92 us (3%)
  between operations  0.65 us (1%)
    pallas_call x1, Pallas kernels, on_device(): pl.pallas_call(kernel, out_shape=(jax.ShapeDtypeStruct((32, B), F32), jax...  58.6 us
    unnamed x4, local copies, waits for them, and re-layouts  1.92 us

profile of v2, /device:TPU:1, one launch (start us, length us, event | category | flops | bytes accessed | tf_op | source)
XLA Modules:
  0.0 61.1 jit_solution(16052590278070290869)
XLA Ops:
  0.6 58.6 %shard_map.59 = (f32[32,128]{1,0:T(8,128)}, f32[8,128]{1,0:T(8,128)}) custom-call(f32[64,128]{1,0:T(8,128)} %x_ref.1, f32[64,128]{1,0:T(8,128)} %y_ref.1, f32[32,128]{1,0:T(8,128)} %bitcast.5, f32[8,128]{1,0:T(8,128)} %bitcast.7), custom_call_target="tpu_custom_call" | custom-call | tf_op jit(solution)/shard_map/pallas_call | solution.py:305
  59.2 0.0 copy-start
  59.2 1.3 %copy.8 = f32[4096]{0:T(1024)} copy(f32[4096]{0:T(1024)} %bitcast.4) | data formatting | bytes 32768
  60.5 0.0 copy-done
  60.5 0.6 copy.9
Async XLA Ops:
  59.2 1.3 %copy-start = (f32[8,128]{1,0:T(8,128)S(1)}, f32[8,128]{1,0:T(8,128)}, u32[]{:S(2)}) copy-start(f32[8,128]{1,0:T(8,128)} %get-tuple-element.5) | copy-start | bytes 12292

commit v3 on v2

v3 whole, which is shorter than its diff:
```python
import functools
import math

import jax
import jax.numpy as jnp
from jax import lax
from jax.experimental import pallas as pl
from jax.experimental.pallas import tpu as pltpu
from jax.sharding import PartitionSpec as P

MESH = pl.DeviceIdType.MESH
EPSILON = 0.05
LOG2E = math.log2(math.e)
SCORE = LOG2E / EPSILON
UNIT = EPSILON / LOG2E
D = 64
B = 128
NB = 16
N = NB * B
F32 = jnp.float32
BF16 = jnp.bfloat16

PLANE = [(dy, dx) for dy in range(4) for dx in range(4) if (dy, dx) != (0, 0)]
RING = [1, 7, 2, 6, 3, 5, 4]
COLUMN = sorted(
    [(dz, dc) for dz in range(8) for dc in range(2) if (dz, dc) != (0, 0)],
    key=lambda o: min(o[0], 8 - o[0]),
)
FAR = sorted(PLANE, key=lambda o: -min(o[0], 4 - o[0]) - min(o[1], 4 - o[1]))


def lse_rows(values):
    top = jnp.max(values, axis=0)
    return top + jnp.log(jnp.sum(jnp.exp2(values - top[None]), axis=0)) * LOG2E


def tree(op, parts):
    while len(parts) > 1:
        parts = [op(p, q) for p, q in zip(parts[::2], parts[1::2])]
    return parts[0]


def kernel(
    x_ref, y_ref, a_ref, b_ref, f_ref, g_ref,
    xs, ys, av, bown, bsib, X, Y, T, MS, xn, yn, gb, ba, fa, fb8, mbuf, sbuf, R8, v8,
    ex1, ex2, ex3, ex4, fsib,
    in_sem, x_send, x_recv, y_send, y_recv, p_send, p_recv, b_sem, e_send, e_recv, f_sem,
):
    z = lax.axis_index("row")
    c = lax.axis_index("col")
    core = lax.rem(c, 2)
    chip = lax.div(c, 2)
    xi = lax.rem(chip, 4)
    yi = lax.div(chip, 4)
    here = core * 8 + z

    def plane(o):
        dy, dx = o
        return (z, (lax.rem(yi + dy, 4) * 4 + lax.rem(xi + dx, 4)) * 2 + core)

    def column(o):
        dz, dc = o
        return (lax.rem(z + dz, 8), chip * 2 + lax.rem(core + dc, 2))

    def source_row(k):
        dy, dx = lax.div(k, 4), lax.rem(k, 4)
        return lax.rem(yi + 4 - dy, 4) * 4 + lax.rem(xi + 4 - dx, 4)

    def target_slot(r, dc):
        return (r // 4) * 8 + dc * 4 + r % 4

    def target_row(t):
        r = lax.div(t, 8) * 4 + lax.rem(t, 4)
        dc = lax.rem(lax.div(t, 4), 2)
        odd = lax.rem(r, 2)
        dz = odd * lax.div(r + 1, 2) + (1 - odd) * (8 - lax.div(r, 2))
        return lax.rem(core + dc, 2) * 8 + lax.rem(z + 16 - dz, 8)

    sibling = column((0, 1))

    def send(src, dst, ssem, rsem, dev):
        copy = pltpu.make_async_remote_copy(
            src_ref=src, dst_ref=dst, send_sem=ssem, recv_sem=rsem, device_id=dev, device_id_type=MESH
        )
        copy.start()

    def wait(ref, sem):
        pltpu.make_async_copy(ref, ref, sem).wait()

    barrier = pltpu.get_barrier_semaphore()
    for o in PLANE:
        pl.semaphore_signal(barrier, inc=1, device_id=plane(o), device_id_type=MESH)
    for o in COLUMN:
        pl.semaphore_signal(barrier, inc=1, device_id=column(o), device_id_type=MESH)
    loads = [
        pltpu.make_async_copy(src, dst, in_sem.at[k])
        for k, (src, dst) in enumerate([(x_ref, xs.at[0]), (y_ref, ys.at[0]), (b_ref, bown), (a_ref, av)])
    ]
    for load in loads:
        load.start()
    ones = (lax.broadcasted_iota(jnp.int32, (D, B), 0) < 3).astype(BF16)
    left = lax.broadcasted_iota(jnp.int32, (B, B), 1) < D
    for load in loads:
        load.wait()
    pl.semaphore_wait(barrier, len(PLANE) + len(COLUMN))

    def send_points(e, rings, slots):
        for r in rings:
            send(ys.at[0], ys.at[target_slot(r, 0)], y_send.at[e], y_recv.at[r], column((RING[r - 1], 0)))
        for k in slots:
            send(xs.at[0], xs.at[k], x_send.at[e], x_recv.at[k], plane((k // 4, k % 4)))

    send_points(0, (1, 2, 3), range(1, 8))
    send(ys.at[0], ys.at[target_slot(0, 1)], p_send, p_recv.at[0], sibling)
    send(bown, bsib, b_sem.at[0], b_sem.at[1], sibling)
    wait(ys.at[pl.ds(0, 3)], y_send.at[0])
    wait(xs.at[pl.ds(0, 7)], x_send.at[0])
    send_points(1, (4, 5, 6, 7), range(8, 16))

    def forward(r):
        slot = target_slot(r, 0)
        wait(ys.at[slot], y_recv.at[r])
        send(ys.at[slot], ys.at[target_slot(r, 1)], p_send, p_recv.at[r], sibling)

    def build_source(k):
        x = xs[k]
        xn[pl.ds(source_row(k), 1), :] = jnp.sum(x * x, axis=0, keepdims=True)
        scaled = x * (2.0 * SCORE)
        hi = scaled.astype(BF16)
        lo = (scaled - hi.astype(F32)).astype(BF16)
        at = slice(k * B, k * B + B)
        X[0:64, at] = hi
        X[64:128, at] = ones
        X[128:192, at] = hi
        X[192:256, at] = lo

    def build_target(t):
        y = ys[t]
        row = target_row(t)
        norm = jnp.sum(y * y, axis=0, keepdims=True)
        yn[pl.ds(row, 1), :] = norm
        mass = (bsib if t % 8 >= 4 else bown)[pl.ds(lax.rem(row, 8), 1), :] * LOG2E
        ba[pl.ds(row, 1), :] = mass
        bias = mass - norm * SCORE
        gb[pl.ds(row, 1), :] = bias
        hi = bias.astype(BF16).astype(F32)
        mid = (bias - hi).astype(BF16).astype(F32)
        lo = bias - hi - mid
        at8 = lax.broadcasted_iota(jnp.int32, (D, B), 0)
        tail = jnp.where(at8 == 0, hi, jnp.where(at8 == 1, mid, jnp.where(at8 == 2, lo, 0.0)))
        both = jnp.concatenate([y, tail], axis=0).T
        top = both.astype(BF16).astype(F32)
        rest = jnp.where(left, both - top, pltpu.roll(top, D, 1))
        at = slice(t * B, t * B + B)
        Y[at, 0:128] = top.astype(BF16)
        Y[at, 128:256] = rest.astype(BF16)

    def scores(r0, rn, c0, cn, fresh):
        step = 256

        def chunk(n, _):
            at = pl.ds(pl.multiple_of(c0 + n * 2 * step, 2 * step), 2 * step)
            Tb = T.at[r0 : r0 + rn, at]
            Mb, Sb = MS.at[0, :, at], MS.at[1, :, at]
            Xb = X.at[:, at]
            for h in range(2):
                half = slice(h * step, h * step + step)
                Tb[:, half] = jnp.dot(Y[r0 : r0 + rn, :], Xb[:, half], preferred_element_type=F32)
            for u in range(2 * step // B):
                lane = slice(u * B, u * B + B)
                m = s = None
                if not fresh:
                    m, s = Mb[:, lane], Sb[:, lane]
                for q in range(rn // B):
                    rows = [Tb[q * B + r * 8 : q * B + r * 8 + 8, lane] for r in range(16)]
                    new = tree(jnp.maximum, rows)
                    if m is not None:
                        new = jnp.maximum(m, new)
                    total = tree(jnp.add, [jnp.exp2(r - new) for r in rows])
                    s = total if m is None else total + s * jnp.exp2(m - new)
                    m = new
                Mb[:, lane] = m
                Sb[:, lane] = s
            return 0

        lax.fori_loop(0, cn // (2 * step), chunk, 0)

    H = N // 2
    Q = N // 4
    for r in (1, 2, 3):
        forward(r)
    for k in range(1, 8):
        wait(xs.at[k], x_recv.at[k])
    wait(bsib, b_sem.at[1])
    for k in range(8):
        build_source(k)
    for t in range(4):
        build_target(t)
    scores(0, Q, 0, H, True)
    for r in range(4):
        wait(ys.at[0], p_recv.at[r])
    for t in range(4, 8):
        build_target(t)
    scores(Q, Q, 0, H, False)
    for r in (4, 5, 6, 7):
        forward(r)
    for k in range(8, 16):
        wait(xs.at[k], x_recv.at[k])
    for k in range(8, 16):
        build_source(k)
    scores(0, H, H, H, True)
    for t in range(8, 12):
        build_target(t)
    scores(H, Q, 0, N, False)
    for r in range(4, 8):
        wait(ys.at[0], p_recv.at[r])
    for t in range(12, 16):
        build_target(t)
    scores(H + Q, Q, 0, N, False)
    for k in range(NB):
        lane = slice(k * B, k * B + B)
        m, s = MS[0, :, lane], MS[1, :, lane]
        top = jnp.max(m, axis=0, keepdims=True)
        total = jnp.sum(s * jnp.exp2(m - top), axis=0, keepdims=True)
        ex1[chip, pl.ds(source_row(k), 1), :] = top + jnp.log(total) * LOG2E

    def exchange(ex, mine, targets, e):
        for o in targets:
            send(ex.at[mine], ex.at[mine], e_send.at[e], e_recv.at[e], o)
        wait(ex.at[pl.ds(0, 15)], e_recv.at[e])

    planes = [plane(o) for o in FAR]
    columns = [column(o) for o in reversed(COLUMN)]

    exchange(ex1, chip, planes, 0)
    a2 = av[pl.ds(core, NB, stride=2), :] * LOG2E
    first = a2 - lse_rows(ex1[...])
    fa[...] = first
    for n in range(NB):
        fb8[:, n * B : (n + 1) * B] = jnp.broadcast_to(fa[pl.ds(source_row(n), 1), :], (8, B))

    def half2(t, _):
        block = pl.ds(pl.multiple_of(t * B, B), B)
        Tb, mb, sb = T.at[block], mbuf.at[block], sbuf.at[block]
        for q in range(NB):
            at = slice(q * 8, q * 8 + 8)
            parts = []
            for n in range(NB):
                lane = slice(n * B, (n + 1) * B)
                value = Tb[at, lane] + fb8[:, lane]
                Tb[at, lane] = value
                parts.append(value)
            top = tree(jnp.maximum, parts)
            mb[at, :] = top
            sb[at, :] = tree(jnp.add, [jnp.exp2(p - top) for p in parts])
        return 0

    lax.fori_loop(0, NB, half2, 0)

    for t in range(NB):
        at = slice(t * B, t * B + B)
        m = mbuf[at, :].T
        s = sbuf[at, :].T
        top = jnp.max(m, axis=0, keepdims=True)
        total = jnp.sum(s * jnp.exp2(m - top), axis=0, keepdims=True)
        ex2[here, pl.ds(target_row(t), 1), :] = top + jnp.log(total) * LOG2E

    exchange(ex2, here, columns, 1)
    b2 = ba[...]
    total2 = lse_rows(ex2[...])
    gb[...] = gb[...] - total2 + b2
    fa[...] = b2 - total2

    R8[...] = jnp.zeros((8, N), F32)

    for t in range(NB):
        mbuf[t * B : t * B + B, :] = jnp.broadcast_to(fa[pl.ds(target_row(t), 1), :], (B, B)).T

    def half3(t, _):
        block = pl.ds(pl.multiple_of(t * B, B), B)
        Tb, mb = T.at[block], mbuf.at[block]
        for h in range(2):
            ats = [slice((h * 8 + q) * 8, (h * 8 + q) * 8 + 8) for q in range(8)]
            shifts = [mb[at, :] for at in ats]
            for n in range(NB):
                lane = slice(n * B, (n + 1) * B)
                values = []
                for at, shift in zip(ats, shifts):
                    value = jnp.exp2(Tb[at, lane] + shift)
                    Tb[at, lane] = value
                    values.append(value)
                R8[:, lane] = R8[:, lane] + tree(jnp.add, values)
        return 0

    lax.fori_loop(0, NB, half3, 0)
    for n in range(NB):
        ex3[chip, pl.ds(source_row(n), 1), :] = jnp.sum(R8[:, n * B : (n + 1) * B], axis=0, keepdims=True)
    exchange(ex3, chip, planes, 2)
    total3 = jnp.sum(ex3[...], axis=0)
    second = first - jnp.log(total3) * LOG2E
    fsib[0] = xn[...] + second * UNIT
    send(fsib.at[0], fsib.at[1], f_sem.at[0], f_sem.at[1], sibling)
    fa[...] = jnp.exp2(a2) / total3
    for n in range(NB):
        v8[:, n * B : (n + 1) * B] = jnp.broadcast_to(fa[pl.ds(source_row(n), 1), :], (8, B))

    def half4(t, _):
        block = pl.ds(pl.multiple_of(t * B, B), B)
        Tb, sb = T.at[block], sbuf.at[block]
        for h in range(2):
            ats = [slice((h * 8 + q) * 8, (h * 8 + q) * 8 + 8) for q in range(8)]
            sums = [None] * 8
            for n in range(NB):
                lane = slice(n * B, (n + 1) * B)
                weight = v8[:, lane]
                for q, at in enumerate(ats):
                    value = Tb[at, lane] * weight
                    sums[q] = value if n == 0 else sums[q] + value
            for q, at in enumerate(ats):
                sb[at, :] = sums[q]
        return 0

    lax.fori_loop(0, NB, half4, 0)

    for t in range(NB):
        total = jnp.sum(sbuf[t * B : t * B + B, :].T, axis=0, keepdims=True)
        ex4[here, pl.ds(target_row(t), 1), :] = total

    exchange(ex4, here, columns, 3)
    total4 = jnp.sum(ex4[...], axis=0)
    fa[...] = yn[...] + (gb[...] - jnp.log(total4) * LOG2E) * UNIT
    g_ref[...] = fa[pl.ds(pl.multiple_of(core * 8, 8), 8), :]
    wait(fsib.at[1], f_sem.at[1])
    f_ref[pl.ds(core, NB, stride=2), :] = fsib[0]
    f_ref[pl.ds(1 - core, NB, stride=2), :] = fsib[1]

    wait(xs.at[pl.ds(0, 8)], x_send.at[1])
    wait(ys.at[pl.ds(0, 4)], y_send.at[1])
    wait(ys.at[pl.ds(0, 8)], p_send)
    wait(bown, b_sem.at[0])
    wait(fsib.at[0], f_sem.at[0])
    for e, ex in enumerate((ex1, ex2, ex3, ex4)):
        wait(ex.at[pl.ds(0, 15)], e_send.at[e])


def on_device(src_points, tgt_points, src_logmass, tgt_logmass):
    vmem = pl.BlockSpec(memory_space=pltpu.VMEM)
    dma = pltpu.SemaphoreType.DMA
    exchange = pltpu.VMEM((NB, NB, B), F32)
    f, g = pl.pallas_call(
        kernel,
        out_shape=(jax.ShapeDtypeStruct((32, B), F32), jax.ShapeDtypeStruct((8, B), F32)),
        in_specs=[pl.BlockSpec(memory_space=pl.ANY)] * 4,
        out_specs=(vmem, vmem),
        scratch_shapes=[
            pltpu.VMEM((NB, D, B), F32),
            pltpu.VMEM((NB, D, B), F32),
            pltpu.VMEM((32, B), F32),
            pltpu.VMEM((8, B), F32),
            pltpu.VMEM((8, B), F32),
            pltpu.VMEM((256, N), BF16),
            pltpu.VMEM((N, 256), BF16),
            pltpu.VMEM((N, N), F32),
            pltpu.VMEM((2, 8, N), F32),
            pltpu.VMEM((NB, B), F32),
            pltpu.VMEM((NB, B), F32),
            pltpu.VMEM((NB, B), F32),
            pltpu.VMEM((NB, B), F32),
            pltpu.VMEM((NB, B), F32),
            pltpu.VMEM((8, N), F32),
            pltpu.VMEM((N, B), F32),
            pltpu.VMEM((N, B), F32),
            pltpu.VMEM((8, N), F32),
            pltpu.VMEM((8, N), F32),
            exchange, exchange, exchange, exchange,
            pltpu.VMEM((2, NB, B), F32),
            dma((4,)), dma((2,)), dma((16,)), dma((2,)), dma((8,)), dma, dma((8,)), dma((2,)), dma((4,)), dma((4,)), dma((2,)),
        ],
        compiler_params=pltpu.CompilerParams(
            collective_id=0, has_side_effects=True, vmem_limit_bytes=56 << 20
        ),
    )(src_points, tgt_points, src_logmass.reshape(32, B), tgt_logmass.reshape(8, B))
    return f.reshape(-1), g.reshape(-1)


def solution(mesh):
    return jax.shard_map(
        on_device,
        mesh=mesh,
        in_specs=(P(None, ("row", "col")), P(None, ("col", "row")), P("row"), P("col")),
        out_specs=(P("row"), P("col")),
        check_vma=False,
    )
```

time: 61.3 us -> 57.4 us (0.936)
  Pallas kernels: 58.6 us -> 54.7 us
    pallas_call x1, Pallas kernels: 58.6 us -> 54.7 us  [on_device(): pl.pallas_call(kernel, out_shape=(jax.ShapeDtypeStruct((32, B), F32), jax...]
where the time goes in v3:
time: 57.4 us; the launch traced here: 57.2 us
  Pallas kernels  54.7 us (95%)
  local copies, waits for them, and re-layouts  1.92 us (3%)
  between operations  0.65 us (1%)
    pallas_call x1, Pallas kernels, on_device(): pl.pallas_call(kernel, out_shape=(jax.ShapeDtypeStruct((32, B), F32), jax...  54.7 us
    unnamed x4, local copies, waits for them, and re-layouts  1.92 us

profile of v3, /device:TPU:1, one launch (start us, length us, event | category | flops | bytes accessed | tf_op | source)
XLA Modules:
  0.0 57.2 jit_solution(14637421278351524296)
XLA Ops:
  0.6 54.7 %shard_map.59 = (f32[32,128]{1,0:T(8,128)}, f32[8,128]{1,0:T(8,128)}) custom-call(f32[64,128]{1,0:T(8,128)} %x_ref.1, f32[64,128]{1,0:T(8,128)} %y_ref.1, f32[32,128]{1,0:T(8,128)} %bitcast.5, f32[8,128]{1,0:T(8,128)} %bitcast.7), custom_call_target="tpu_custom_call" | custom-call | tf_op jit(solution)/shard_map/pallas_call | solution.py:350
  55.3 0.0 copy-start
  55.3 1.3 %copy.8 = f32[4096]{0:T(1024)} copy(f32[4096]{0:T(1024)} %bitcast.4) | data formatting | bytes 32768
  56.6 0.0 copy-done
  56.7 0.6 %copy.9 = f32[1024]{0:T(1024)} copy(f32[1024]{0:T(1024)S(1)} %bitcast.6) | data formatting | bytes 8192
Async XLA Ops:
  55.3 1.3 %copy-start = (f32[8,128]{1,0:T(8,128)S(1)}, f32[8,128]{1,0:T(8,128)}, u32[]{:S(2)}) copy-start(f32[8,128]{1,0:T(8,128)} %get-tuple-element.5) | copy-start | bytes 12292

commit v4 on v3

--- a/solution.py
+++ b/solution.py
@@ -157,16 +157,17 @@
 
     def scores(r0, rn, c0, cn, fresh):
         step = 256
+        width = cn // 2
 
         def chunk(n, _):
-            at = pl.ds(pl.multiple_of(c0 + n * 2 * step, 2 * step), 2 * step)
+            at = pl.ds(pl.multiple_of(c0 + n * width, width), width)
             Tb = T.at[r0 : r0 + rn, at]
             Mb, Sb = MS.at[0, :, at], MS.at[1, :, at]
             Xb = X.at[:, at]
-            for h in range(2):
+            for h in range(width // step):
                 half = slice(h * step, h * step + step)
                 Tb[:, half] = jnp.dot(Y[r0 : r0 + rn, :], Xb[:, half], preferred_element_type=F32)
-            for u in range(2 * step // B):
+            for u in range(width // B):
                 lane = slice(u * B, u * B + B)
                 m = s = None
                 if not fresh:
@@ -183,7 +184,7 @@
                 Sb[:, lane] = s
             return 0
 
-        lax.fori_loop(0, cn // (2 * step), chunk, 0)
+        lax.fori_loop(0, 2, chunk, 0)
 
     H = N // 2
     Q = N // 4

time: 57.4 us -> 57 us (level)
  no operation moved by 1% of the time
where the time goes in v4:
time: 57 us; the launch traced here: 56.8 us
  Pallas kernels  54.2 us (95%)
  local copies, waits for them, and re-layouts  1.92 us (3%)
  between operations  0.65 us (1%)
    pallas_call x1, Pallas kernels, on_device(): pl.pallas_call(kernel, out_shape=(jax.ShapeDtypeStruct((32, B), F32), jax...  54.2 us
    unnamed x4, local copies, waits for them, and re-layouts  1.92 us

profile of v4, /device:TPU:1, one launch (start us, length us, event | category | flops | bytes accessed | tf_op | source)
XLA Modules:
  0.0 56.8 jit_solution(8029069645708247582)
XLA Ops:
  0.6 54.2 %shard_map.59 = (f32[32,128]{1,0:T(8,128)}, f32[8,128]{1,0:T(8,128)}) custom-call(f32[64,128]{1,0:T(8,128)} %x_ref.1, f32[64,128]{1,0:T(8,128)} %y_ref.1, f32[32,128]{1,0:T(8,128)} %bitcast.5, f32[8,128]{1,0:T(8,128)} %bitcast.7), custom_call_target="tpu_custom_call" | custom-call | tf_op jit(solution)/shard_map/pallas_call | solution.py:351
  54.9 0.0 copy-start
  54.9 1.3 %copy.8 = f32[4096]{0:T(1024)} copy(f32[4096]{0:T(1024)} %bitcast.4) | data formatting | bytes 32768
  56.2 0.0 copy-done
  56.2 0.6 %copy.9 = f32[1024]{0:T(1024)} copy(f32[1024]{0:T(1024)S(1)} %bitcast.6) | data formatting | bytes 8192
Async XLA Ops:
  54.9 1.3 %copy-start = (f32[8,128]{1,0:T(8,128)S(1)}, f32[8,128]{1,0:T(8,128)}, u32[]{:S(2)}) copy-start(f32[8,128]{1,0:T(8,128)} %get-tuple-element.5) | copy-start | bytes 12292

commit v5 on v4

--- a/solution.py
+++ b/solution.py
@@ -44,7 +44,7 @@
     x_ref, y_ref, a_ref, b_ref, f_ref, g_ref,
     xs, ys, av, bown, bsib, X, Y, T, MS, xn, yn, gb, ba, fa, fb8, mbuf, sbuf, R8, v8,
     ex1, ex2, ex3, ex4, fsib,
-    in_sem, x_send, x_recv, y_send, y_recv, p_send, p_recv, b_sem, e_send, e_recv, f_sem,
+    in_sem, x_send, x_recv, y_send, y_recv, p_send, p_recv, b_sem, e_send, e_recv, r_send, r_recv, f_sem,
 ):
     z = lax.axis_index("row")
     c = lax.axis_index("col")
@@ -277,51 +277,74 @@
     for t in range(NB):
         mbuf[t * B : t * B + B, :] = jnp.broadcast_to(fa[pl.ds(target_row(t), 1), :], (B, B)).T
 
-    def half3(t, _):
-        block = pl.ds(pl.multiple_of(t * B, B), B)
-        Tb, mb = T.at[block], mbuf.at[block]
-        for h in range(2):
-            ats = [slice((h * 8 + q) * 8, (h * 8 + q) * 8 + 8) for q in range(8)]
-            shifts = [mb[at, :] for at in ats]
-            for n in range(NB):
-                lane = slice(n * B, (n + 1) * B)
-                values = []
-                for at, shift in zip(ats, shifts):
-                    value = jnp.exp2(Tb[at, lane] + shift)
-                    Tb[at, lane] = value
-                    values.append(value)
-                R8[:, lane] = R8[:, lane] + tree(jnp.add, values)
-        return 0
-
-    lax.fori_loop(0, NB, half3, 0)
-    for n in range(NB):
-        ex3[chip, pl.ds(source_row(n), 1), :] = jnp.sum(R8[:, n * B : (n + 1) * B], axis=0, keepdims=True)
-    exchange(ex3, chip, planes, 2)
-    total3 = jnp.sum(ex3[...], axis=0)
-    second = first - jnp.log(total3) * LOG2E
-    fsib[0] = xn[...] + second * UNIT
-    send(fsib.at[0], fsib.at[1], f_sem.at[0], f_sem.at[1], sibling)
-    fa[...] = jnp.exp2(a2) / total3
-    for n in range(NB):
-        v8[:, n * B : (n + 1) * B] = jnp.broadcast_to(fa[pl.ds(source_row(n), 1), :], (8, B))
-
-    def half4(t, _):
-        block = pl.ds(pl.multiple_of(t * B, B), B)
-        Tb, sb = T.at[block], sbuf.at[block]
-        for h in range(2):
-            ats = [slice((h * 8 + q) * 8, (h * 8 + q) * 8 + 8) for q in range(8)]
-            sums = [None] * 8
-            for n in range(NB):
-                lane = slice(n * B, (n + 1) * B)
-                weight = v8[:, lane]
+    def lanes_of(my):
+        return pl.ds(pl.multiple_of(lax.rem(yi + 4 - my, 4) * Q, Q), Q)
+
+    for e in range(2):
+        spans = [lanes_of(2 * e), lanes_of(2 * e + 1)]
+
+        def half3(t, _):
+            block = pl.ds(pl.multiple_of(t * B, B), B)
+            mb = mbuf.at[block]
+            for span in spans:
+                Tb, Rb = T.at[block, span], R8.at[:, span]
+                for h in range(2):
+                    ats = [slice((h * 8 + q) * 8, (h * 8 + q) * 8 + 8) for q in range(8)]
+                    shifts = [mb[at, :] for at in ats]
+                    for n in range(4):
+                        lane = slice(n * B, (n + 1) * B)
+                        values = []
+                        for at, shift in zip(ats, shifts):
+                            value = jnp.exp2(Tb[at, lane] + shift)
+                            Tb[at, lane] = value
+                            values.append(value)
+                        Rb[:, lane] = Rb[:, lane] + tree(jnp.add, values)
+            return 0
+
+        lax.fori_loop(0, NB, half3, 0)
+        for g, span in enumerate(spans):
+            Rb = R8.at[:, span]
+            for n in range(4):
+                row = (2 * e + g) * 4 + lax.rem(xi + 4 - n, 4)
+                ex3[chip, pl.ds(row, 1), :] = jnp.sum(Rb[:, n * B : (n + 1) * B], axis=0, keepdims=True)
+        part = ex3.at[chip, pl.ds(8 * e, 8)]
+        for o in planes:
+            send(part, part, r_send.at[e], r_recv.at[e], o)
+
+    for e in range(2):
+        wait(ex3.at[pl.ds(0, 15), pl.ds(0, 8)], r_recv.at[e])
+        rows = slice(8 * e, 8 * e + 8)
+        total3 = jnp.sum(ex3[:, rows, :], axis=0)
+        fsib[0, rows, :] = xn[rows, :] + (first[rows] - jnp.log(total3) * LOG2E) * UNIT
+        fa[rows, :] = jnp.exp2(a2[rows]) / total3
+        spans = [lanes_of(2 * e), lanes_of(2 * e + 1)]
+        for g, span in enumerate(spans):
+            vb = v8.at[:, span]
+            for n in range(4):
+                row = (2 * e + g) * 4 + lax.rem(xi + 4 - n, 4)
+                vb[:, n * B : (n + 1) * B] = jnp.broadcast_to(fa[pl.ds(row, 1), :], (8, B))
+        if e == 1:
+            send(fsib.at[0], fsib.at[1], f_sem.at[0], f_sem.at[1], sibling)
+
+        def half4(t, _):
+            block = pl.ds(pl.multiple_of(t * B, B), B)
+            sb = sbuf.at[block]
+            for h in range(2):
+                ats = [slice((h * 8 + q) * 8, (h * 8 + q) * 8 + 8) for q in range(8)]
+                sums = [sb[at, :] for at in ats] if e else [None] * 8
+                for span in spans:
+                    Tb, vb = T.at[block, span], v8.at[:, span]
+                    for n in range(4):
+                        lane = slice(n * B, (n + 1) * B)
+                        weight = vb[:, lane]
+                        for q, at in enumerate(ats):
+                            value = Tb[at, lane] * weight
+                            sums[q] = value if sums[q] is None else sums[q] + value
                 for q, at in enumerate(ats):
-                    value = Tb[at, lane] * weight
-                    sums[q] = value if n == 0 else sums[q] + value
-            for q, at in enumerate(ats):
-                sb[at, :] = sums[q]
-        return 0
-
-    lax.fori_loop(0, NB, half4, 0)
+                    sb[at, :] = sums[q]
+            return 0
+
+        lax.fori_loop(0, NB, half4, 0)
 
     for t in range(NB):
         total = jnp.sum(sbuf[t * B : t * B + B, :].T, axis=0, keepdims=True)
@@ -340,7 +363,9 @@
     wait(ys.at[pl.ds(0, 8)], p_send)
     wait(bown, b_sem.at[0])
     wait(fsib.at[0], f_sem.at[0])
-    for e, ex in enumerate((ex1, ex2, ex3, ex4)):
+    for e in range(2):
+        wait(ex3.at[pl.ds(0, 15), pl.ds(0, 8)], r_send.at[e])
+    for e, ex in ((0, ex1), (1, ex2), (3, ex4)):
         wait(ex.at[pl.ds(0, 15)], e_send.at[e])
 
 
@@ -375,7 +400,7 @@
             pltpu.VMEM((8, N), F32),
             exchange, exchange, exchange, exchange,
             pltpu.VMEM((2, NB, B), F32),
-            dma((4,)), dma((2,)), dma((16,)), dma((2,)), dma((8,)), dma, dma((8,)), dma((2,)), dma((4,)), dma((4,)), dma((2,)),
+            dma((4,)), dma((2,)), dma((16,)), dma((2,)), dma((8,)), dma, dma((8,)), dma((2,)), dma((4,)), dma((4,)), dma((2,)), dma((2,)), dma((2,)),
         ],
         compiler_params=pltpu.CompilerParams(
             collective_id=0, has_side_effects=True, vmem_limit_bytes=56 << 20

time: 57 us -> 56.7 us (level)
  no operation moved by 1% of the time
where the time goes in v5:
time: 56.7 us; the launch traced here: 56.5 us
  Pallas kernels  53.9 us (95%)
  local copies, waits for them, and re-layouts  1.92 us (3%)
  between operations  0.65 us (1%)
    pallas_call x1, Pallas kernels, on_device(): pl.pallas_call(kernel, out_shape=(jax.ShapeDtypeStruct((32, B), F32), jax...  53.9 us
    unnamed x4, local copies, waits for them, and re-layouts  1.92 us

profile of v5, /device:TPU:1, one launch (start us, length us, event | category | flops | bytes accessed | tf_op | source)
XLA Modules:
  0.0 56.5 jit_solution(4008731717682549129)
XLA Ops:
  0.6 53.9 %shard_map.59 = (f32[32,128]{1,0:T(8,128)}, f32[8,128]{1,0:T(8,128)}) custom-call(f32[64,128]{1,0:T(8,128)} %x_ref.1, f32[64,128]{1,0:T(8,128)} %y_ref.1, f32[32,128]{1,0:T(8,128)} %bitcast.5, f32[8,128]{1,0:T(8,128)} %bitcast.7), custom_call_target="tpu_custom_call" | custom-call | tf_op jit(solution)/shard_map/pallas_call | solution.py:376
  54.5 0.0 copy-start
  54.5 1.3 %copy.8 = f32[4096]{0:T(1024)} copy(f32[4096]{0:T(1024)} %bitcast.4) | data formatting | bytes 32768
  55.9 0.0 copy-done
  55.9 0.6 %copy.9 = f32[1024]{0:T(1024)} copy(f32[1024]{0:T(1024)S(1)} %bitcast.6) | data formatting | bytes 8192
Async XLA Ops:
  54.5 1.3 %copy-start = (f32[8,128]{1,0:T(8,128)S(1)}, f32[8,128]{1,0:T(8,128)}, u32[]{:S(2)}) copy-start(f32[8,128]{1,0:T(8,128)} %get-tuple-element.5) | copy-start | bytes 12292

commit v6 on v5

--- a/solution.py
+++ b/solution.py
@@ -114,8 +114,9 @@
     send(ys.at[0], ys.at[target_slot(0, 1)], p_send, p_recv.at[0], sibling)
     send(bown, bsib, b_sem.at[0], b_sem.at[1], sibling)
     wait(ys.at[pl.ds(0, 3)], y_send.at[0])
+    send_points(1, (4, 5, 6, 7), ())
     wait(xs.at[pl.ds(0, 7)], x_send.at[0])
-    send_points(1, (4, 5, 6, 7), range(8, 16))
+    send_points(1, (), range(8, 16))
 
     def forward(r):
         slot = target_slot(r, 0)

time: 56.7 us -> 57.1 us (level)
  no operation moved by 1% of the time
where the time goes in v6:
time: 57.1 us; the launch traced here: 56.9 us
  Pallas kernels  54.3 us (95%)
  local copies, waits for them, and re-layouts  1.92 us (3%)
  between operations  0.65 us (1%)
    pallas_call x1, Pallas kernels, on_device(): pl.pallas_call(kernel, out_shape=(jax.ShapeDtypeStruct((32, B), F32), jax...  54.3 us
    unnamed x4, local copies, waits for them, and re-layouts  1.92 us

profile of v6, /device:TPU:1, one launch (start us, length us, event | category | flops | bytes accessed | tf_op | source)
XLA Modules:
  0.0 56.9 jit_solution(9665278882937723398)
XLA Ops:
  0.6 54.3 %shard_map.59 = (f32[32,128]{1,0:T(8,128)}, f32[8,128]{1,0:T(8,128)}) custom-call(f32[64,128]{1,0:T(8,128)} %x_ref.1, f32[64,128]{1,0:T(8,128)} %y_ref.1, f32[32,128]{1,0:T(8,128)} %bitcast.5, f32[8,128]{1,0:T(8,128)} %bitcast.7), custom_call_target="tpu_custom_call" | custom-call | tf_op jit(solution)/shard_map/pallas_call | solution.py:377
  54.9 0.0 copy-start
  55.0 1.3 %copy.8 = f32[4096]{0:T(1024)} copy(f32[4096]{0:T(1024)} %bitcast.4) | data formatting | bytes 32768
  56.3 0.0 copy-done
  56.3 0.6 %copy.9 = f32[1024]{0:T(1024)} copy(f32[1024]{0:T(1024)S(1)} %bitcast.6) | data formatting | bytes 8192
Async XLA Ops:
  54.9 1.3 %copy-start = (f32[8,128]{1,0:T(8,128)S(1)}, f32[8,128]{1,0:T(8,128)}, u32[]{:S(2)}) copy-start(f32[8,128]{1,0:T(8,128)} %get-tuple-element.5) | copy-start | bytes 12292
